TPU v7x, 32 devices: a whole 2x2x4 slice. The times are simulated.
32 devices in a mesh: fsdp: 8 (over y, x, core), tp: 4 (over z).
Axes of the slice: x: 2, y: 2, z: 4, core: 2. Of those that a mesh axis runs over, the one named last changes fastest.
Arguments:
- tokens: bfloat16 [16, 8192], P('fsdp', 'tp'), may hold values from -6 to 6
- gate_weight: bfloat16 [27648, 8192], P('fsdp', 'tp'), may hold values from -0.0625 to 0.0625
- up_weight: bfloat16 [27648, 8192], P('fsdp', 'tp'), may hold values from -0.0625 to 0.0625
- down_weight: bfloat16 [27648, 8192], P('fsdp', 'tp'), may hold values from -0.0390625 to 0.0390625
Outputs:
- mixed: bfloat16 [16, 8192], P('fsdp', 'tp')
All inputs are finite; a program needn't handle non-finite values.
Results may differ from a plain program's by a relative error of at most 0.0049.
Values may be sent and summed in bfloat16 or wider, within the bound.
A program may use at most 128 MiB of HBM per device.

v0:
```python
import jax
import jax.numpy as jnp
from jax import lax
from jax.sharding import PartitionSpec as P


def body(tokens, gate_weight, up_weight, down_weight):
    hidden_width = gate_weight.shape[0]
    contract = (((1,), (1,)), ((), ()))
    block_rows = lax.all_gather(tokens, "fsdp", axis=0, tiled=True)
    gate_part = lax.dot_general(
        block_rows, gate_weight, contract, preferred_element_type=jnp.float32
    )
    up_part = lax.dot_general(block_rows, up_weight, contract, preferred_element_type=jnp.float32)
    partial_value = jnp.concatenate([gate_part, up_part], axis=1)
    share_rows = lax.psum_scatter(partial_value, "tp", scatter_dimension=0, tiled=True)
    quarter = (jax.nn.silu(share_rows[:, :hidden_width]) * share_rows[:, hidden_width:]).astype(
        jnp.bfloat16
    )
    hidden = lax.all_gather(quarter, "tp", axis=0, tiled=True)
    down_terms = jnp.dot(hidden, down_weight, preferred_element_type=jnp.float32)
    mixed = lax.psum_scatter(down_terms, "fsdp", scatter_dimension=0, tiled=True)
    return mixed.astype(jnp.bfloat16)


def solution(mesh):
    placed = (P("fsdp", "tp"), P("fsdp", "tp"), P("fsdp", "tp"), P("fsdp", "tp"))
    return jax.shard_map(
        body, mesh=mesh, in_specs=placed, out_specs=P("fsdp", "tp"), check_vma=False
    )
```

profile of v0, /device:TPU:0, one launch (start us, length us, event | category | flops | bytes accessed | tf_op | source)
XLA Modules:
  0.0 121.2 jit_solution(12058983761775770640)
XLA Ops:
  6.5 0.0 all-reduce.5.cloned.1.call-start
  6.5 10.8 %all-gather = bf16[8,2,2048]{2,1,0:T(2,128)(2,1)S(1)} all-gather(bf16[1,2,2048]{2,1,0:T(2,128)(2,1)} %bitcast.11), channel_id=1, replica_groups=mesh['fsdp'=8,'tp'=4] {'fsdp'}, dimensions={0}, use_global_device_ids=true | all-gather | bytes 73728 | tf_op jit(solution)/shard_map/all_gather | solution.py:10
  17.4 0.0 copy-start
  17.4 8.9 %fusion.3 = f32[16,3456]{1,0:T(8,128)S(1)} fusion(bf16[16,2048]{1,0:T(8,128)(2,1)S(1)} %reshape.1, bf16[3456,2048]{1,0:T(8,128)(2,1)} %param.5), kind=kOutput, calls=%fused_computation.6 | convolution fusion | flops 226492416 | bytes 14442496 | tf_op jit(solution)/shard_map/dot_general | solution.py:11
  26.3 0.1 copy-done
  26.4 3.8 %fusion.4 = f32[16,3456]{1,0:T(8,128)S(1)} fusion(bf16[16,2048]{1,0:T(8,128)(2,1)S(1)} %reshape.1, bf16[3456,2048]{1,0:T(8,128)(2,1)S(1)} %copy-done), kind=kOutput, calls=%fused_computation.7 | convolution fusion | flops 226492416 | bytes 14442496 | tf_op jit(solution)/shard_map/dot_general | solution.py:14
  30.2 0.8 pad_maximum_fusion
  31.0 0.0 all-reduce.5.cloned.1.call-update
  31.0 1.2 %dynamic-slice = u32[1]{0:T(128)} dynamic-slice(u32[32]{0:T(128)} %constant.6, u32[]{:T(128)S(6)} %add.10), dynamic_slice_sizes={1} | dynamic-slice | bytes 12
  32.3 1.2 %dynamic-slice.2 = u32[1]{0:T(128)} dynamic-slice(u32[32]{0:T(128)} %constant.10, u32[]{:T(128)S(6)} %add.10), dynamic_slice_sizes={1} | dynamic-slice | bytes 12
  34.7 34.1 %all-reduce.5.cloned.1.call-done = f32[16,6912]{1,0:T(8,128)} async-done(((f32[16,6912]{1,0:T(8,128)}), f32[16,6912]{1,0:T(8,128)}) %all-reduce.5.cloned.1.call-update) | async-done | bytes 442384
  68.8 1.1 fusion.2
  69.9 13.3 %all-gather.1 = bf16[4,4,3456]{2,1,0:T(4,128)(2,1)S(1)} all-gather(bf16[1,4,3456]{2,1,0:T(4,128)(2,1)S(1)} %fusion.2), channel_id=1, replica_groups=mesh['fsdp'=8,'tp'=4] {'tp'}, dimensions={0}, use_global_device_ids=true | all-gather | bytes 138240 | tf_op jit(solution)/shard_map/all_gather | solution.py:20
  83.2 7.0 %fusion.5 = f32[16,2048]{1,0:T(8,128)S(1)} fusion(bf16[16,3456]{1,0:T(8,128)(2,1)S(1)} %reshape.3, bf16[3456,2048]{1,0:T(8,128)(2,1)} %param.7), kind=kOutput, calls=%fused_computation.8 | convolution fusion | flops 226492416 | bytes 14397440 | tf_op jit(solution)/shard_map/dot_general | solution.py:21
  90.1 23.6 %all-reduce.6 = bf16[16,2048]{1,0:T(8,128)(2,1)S(1)} all-reduce(f32[16,2048]{1,0:T(8,128)S(1)} %fusion.5), channel_id=3, replica_groups=mesh['fsdp'=8,'tp'=4] {'fsdp'}, use_global_device_ids=true, to_apply=%region_1.2.clone | all-reduce | flops 32768 | bytes 196608
  113.8 0.6 dynamic-slice_convert_fusion
  (2 shorter events, 0.1 us)
Async XLA Ops:
  6.5 62.3 %all-reduce.5.cloned.1.call-start = ((), (), s32[]{:S(2)}) async-start(), calls=%async_computation | async-start | bytes 884736
  17.4 9.1 %copy-start = (bf16[3456,2048]{1,0:T(8,128)(2,1)S(1)}, bf16[3456,2048]{1,0:T(8,128)(2,1)}, u32[]{:S(2)}) copy-start(bf16[3456,2048]{1,0:T(8,128)(2,1)} %param.6) | copy-start | bytes 42467332
Sparse Core Ops, SparseCore 0:
  31.2 37.6 all-reduce.4
where the time goes:
time: 122 us; the launch traced here: 121 us
  blocking collectives  47.7 us (39%)
  waiting for transfers between devices  34.1 us (28%)
  matrix products  19.7 us (16%)
  between operations  14.6 us (12%)
  local copies, waits for them, and re-layouts  3.26 us (3%)
  other arithmetic  1.87 us (2%)
    unnamed x2, waiting for transfers between devices  34.1 us
    unnamed x1, blocking collectives  23.6 us
    all_gather x1, blocking collectives, body(): hidden = lax.all_gather(quarter, 'tp', axis=0, tiled=True)  13.3 us
    all_gather x1, blocking collectives, body(): block_rows = lax.all_gather(tokens, 'fsdp', axis=0, tiled=True)  10.8 us
    dot_general x1, matrix products, body(): lax.dot_general(block_rows, gate_weight, contract, preferred_element_type...  8.93 us
    dot_general x1, matrix products, body(): jnp.dot(hidden, down_weight, preferred_element_type=jnp.float32)  6.96 us
    dot_general x1, matrix products, body(): lax.dot_general(block_rows, up_weight, contract, preferred_element_type=j...  3.76 us
    unnamed x6, local copies, waits for them, and re-layouts  2.65 us
  transfers between devices with their start and end apart: 1, of which 1 were waited for; matrix products, arithmetic and copies ran while one was open for 2% of the time, Pallas kernels for 0%

commit v1 on v0

v1 whole, which is shorter than its diff:
```python
import functools

import jax
import jax.numpy as jnp
from jax import lax
from jax.experimental import pallas as pl
from jax.experimental.pallas import tpu as pltpu
from jax.sharding import PartitionSpec as P

MESH = pl.DeviceIdType.MESH
GROUP = 128
LAG = 2
WIRE = jnp.float32
NT = (((1,), (1,)), ((), ()))
VMEM_BYTES = 58 * 2**20


def fused(n_fsdp, n_tp, tokens, gate_w, up_w, down_w, out,
          wg, wu, wd, slots, xf, x, part, own, recv, hid, acc, send, land,
          w_sem, own_sem, tok_send, tok_recv, p_send, p_recv, h_send, h_recv, o_send, o_recv):
    f, t = lax.axis_index("fsdp"), lax.axis_index("tp")
    rows, hidden = tokens.shape[0], gate_w.shape[0]
    chunk = GROUP * n_tp
    n_chunks = -(-hidden // chunk)
    full = hidden // chunk
    last_owners = (hidden - full * chunk) // GROUP

    def width(s):
        return min(chunk, hidden - s * chunk)

    def load(k, source, target, s):
        at = pl.ds(s * chunk, width(s))
        return pltpu.make_async_copy(source.at[at], target.at[at], w_sem.at[k, s])

    for s in range(n_chunks):
        load(0, gate_w, wg, s).start()
        load(1, up_w, wu, s).start()
    for s in range(n_chunks):
        load(2, down_w, wd, s).start()

    own_copy = pltpu.make_async_copy(tokens, slots.at[f], own_sem)
    own_copy.start()

    barrier = pltpu.get_barrier_semaphore()
    for d in range(1, n_fsdp):
        pl.semaphore_signal(barrier, inc=1, device_id={"fsdp": lax.rem(f + d, n_fsdp)}, device_id_type=MESH)
    for d in range(1, n_tp):
        pl.semaphore_signal(barrier, inc=1, device_id={"tp": lax.rem(t + d, n_tp)}, device_id_type=MESH)
    pl.semaphore_wait(barrier, n_fsdp + n_tp - 2)

    def tok_copy(d, slot, peer):
        return pltpu.make_async_remote_copy(
            tokens, slots.at[slot], tok_send.at[d - 1], tok_recv.at[d - 1],
            device_id={"fsdp": peer}, device_id_type=MESH)

    for d in range(1, n_fsdp):
        tok_copy(d, f, lax.rem(f + d, n_fsdp)).start()
    own_copy.wait()
    for d in range(1, n_fsdp):
        tok_copy(d, lax.rem(f + n_fsdp - d, n_fsdp), f).wait_recv()
    for p in range(n_fsdp):
        xf[p * rows:(p + 1) * rows, :] = slots[p].astype(jnp.float32)
    x[...] = xf[...].astype(x.dtype)
    acc[...] = jnp.zeros_like(acc)

    def when(cond, run):
        if cond is True:
            run()
        else:
            pl.when(cond)(run)

    def part_copy(s, d):
        peer = lax.rem(t + d, n_tp)
        return pltpu.make_async_remote_copy(
            part.at[s, peer], recv.at[s, d - 1], p_send.at[s, d - 1], p_recv.at[s, d - 1],
            device_id={"tp": peer}, device_id_type=MESH)

    def hid_copy(s, d, owner):
        return pltpu.make_async_remote_copy(
            hid.at[s, owner], hid.at[s, owner], h_send.at[s, d - 1], h_recv.at[s, d - 1],
            device_id={"tp": lax.rem(t + d, n_tp)}, device_id_type=MESH)

    def gate_up(s, owners):
        size = owners * GROUP
        at = pl.ds(pl.multiple_of(s * chunk, chunk), size)
        for k, (source, target) in enumerate(((gate_w, wg), (up_w, wu))):
            pltpu.make_async_copy(source.at[at], target.at[at], w_sem.at[k, s]).wait()
            sums = lax.dot_general(x[...], target[at, :], NT, preferred_element_type=jnp.float32)
            for j in range(owners):
                piece = sums[:, j * GROUP:(j + 1) * GROUP]
                part[s, j, k] = piece.astype(part.dtype)

                @pl.when(t == j)
                def _():
                    own[s, k] = piece
        for d in range(1, n_tp):
            when(True if owners == n_tp else lax.rem(t + d, n_tp) < owners,
                 lambda d=d: part_copy(s, d).start())

    def activate(s, owners):
        def run():
            gate, up = own[s, 0], own[s, 1]
            for d in range(1, n_tp):
                part_copy(s, d).wait_recv()
                gate = gate + recv[s, d - 1, 0].astype(jnp.float32)
                up = up + recv[s, d - 1, 1].astype(jnp.float32)
            hid[s, t] = (gate / (1.0 + jnp.exp(-gate)) * up).astype(hid.dtype)
            for d in range(1, n_tp):
                hid_copy(s, d, t).start()
        when(True if owners == n_tp else t < owners, run)

    def down(s, owners):
        size = owners * GROUP
        at = pl.ds(pl.multiple_of(s * chunk, chunk), size)
        for d in range(1, n_tp):
            owner = lax.rem(t + n_tp - d, n_tp)
            when(True if owners == n_tp else owner < owners,
                 lambda d=d, owner=owner: hid_copy(s, d, owner).wait_recv())
        pltpu.make_async_copy(down_w.at[at], wd.at[at], w_sem.at[2, s]).wait()
        h = jnp.concatenate([hid[s, j] for j in range(owners)], axis=1)
        acc[...] += jnp.dot(h, wd[at, :], preferred_element_type=jnp.float32)

    @pl.loop(0, full)
    def _(s):
        gate_up(s, n_tp)

        @pl.when(s >= LAG)
        def _():
            activate(s - LAG, n_tp)

    if last_owners:
        gate_up(full, last_owners)

    @pl.loop(full - LAG, full)
    def _(s):
        activate(s, n_tp)

    early = min(2, full)

    @pl.loop(0, early)
    def _(s):
        down(s, n_tp)

    if last_owners:
        activate(full, last_owners)

    @pl.loop(early, full)
    def _(s):
        down(s, n_tp)

    if last_owners:
        down(full, last_owners)

    def out_copy(d, peer):
        return pltpu.make_async_remote_copy(
            send.at[peer], land.at[d - 1], o_send.at[d - 1], o_recv.at[d - 1],
            device_id={"fsdp": peer}, device_id_type=MESH)

    for p in range(n_fsdp):
        send[p] = acc[p * rows:(p + 1) * rows, :]
    for d in range(1, n_fsdp):
        out_copy(d, lax.rem(f + d, n_fsdp)).start()
    total = send[f]
    for d in range(1, n_fsdp):
        out_copy(d, f).wait_recv()
        total = total + land[d - 1]
    out[...] = total.astype(out.dtype)

    for d in range(1, n_fsdp):
        tok_copy(d, f, f).wait_send()
        out_copy(d, f).wait_send()

    @pl.loop(0, full)
    def _(s):
        for d in range(1, n_tp):
            part_copy(s, d).wait_send()
            hid_copy(s, d, t).wait_send()

    if last_owners:
        for d in range(1, n_tp):
            when(lax.rem(t + d, n_tp) < last_owners, lambda d=d: part_copy(full, d).wait_send())
            when(t < last_owners, lambda d=d: hid_copy(full, d, t).wait_send())


def fused_call(n_fsdp, n_tp, tokens, gate_w, up_w, down_w):
    rows, width = tokens.shape
    hidden = gate_w.shape[0]
    chunks = -(-hidden // (GROUP * n_tp))
    every = rows * n_fsdp
    dma = pltpu.SemaphoreType.DMA
    any_spec = pl.BlockSpec(memory_space=pl.ANY)
    return pl.pallas_call(
        functools.partial(fused, n_fsdp, n_tp),
        out_shape=jax.ShapeDtypeStruct((rows, width), tokens.dtype),
        in_specs=[any_spec] * 4,
        out_specs=pl.BlockSpec(memory_space=pltpu.VMEM),
        scratch_shapes=[
            pltpu.VMEM((hidden, width), gate_w.dtype),
            pltpu.VMEM((hidden, width), up_w.dtype),
            pltpu.VMEM((hidden, width), down_w.dtype),
            pltpu.VMEM((n_fsdp, rows, width), tokens.dtype),
            pltpu.VMEM((every, width), jnp.float32),
            pltpu.VMEM((every, width), tokens.dtype),
            pltpu.VMEM((chunks, n_tp, 2, every, GROUP), WIRE),
            pltpu.VMEM((chunks, 2, every, GROUP), jnp.float32),
            pltpu.VMEM((chunks, n_tp - 1, 2, every, GROUP), WIRE),
            pltpu.VMEM((chunks, n_tp, every, GROUP), jnp.bfloat16),
            pltpu.VMEM((every, width), jnp.float32),
            pltpu.VMEM((n_fsdp, rows, width), jnp.float32),
            pltpu.VMEM((n_fsdp - 1, rows, width), jnp.float32),
            dma((3, chunks)),
            dma,
            dma((n_fsdp - 1,)),
            dma((n_fsdp - 1,)),
            dma((chunks, n_tp - 1)),
            dma((chunks, n_tp - 1)),
            dma((chunks, n_tp - 1)),
            dma((chunks, n_tp - 1)),
            dma((n_fsdp - 1,)),
            dma((n_fsdp - 1,)),
        ],
        compiler_params=pltpu.CompilerParams(
            collective_id=0, has_side_effects=True, vmem_limit_bytes=VMEM_BYTES),
        cost_estimate=pl.CostEstimate(
            flops=6 * every * hidden * width, bytes_accessed=6 * hidden * width,
            transcendentals=every * hidden // n_tp),
        name="swiglu",
    )(tokens, gate_w, up_w, down_w)


def collective_body(tokens, gate_weight, up_weight, down_weight):
    hidden_width = gate_weight.shape[0]
    block_rows = lax.all_gather(tokens, "fsdp", axis=0, tiled=True)
    gate_part = lax.dot_general(block_rows, gate_weight, NT, preferred_element_type=jnp.float32)
    up_part = lax.dot_general(block_rows, up_weight, NT, preferred_element_type=jnp.float32)
    partial_value = jnp.concatenate([gate_part, up_part], axis=1)
    share_rows = lax.psum_scatter(partial_value, "tp", scatter_dimension=0, tiled=True)
    quarter = (jax.nn.silu(share_rows[:, :hidden_width]) * share_rows[:, hidden_width:]).astype(
        jnp.bfloat16
    )
    hidden = lax.all_gather(quarter, "tp", axis=0, tiled=True)
    down_terms = jnp.dot(hidden, down_weight, preferred_element_type=jnp.float32)
    mixed = lax.psum_scatter(down_terms, "fsdp", scatter_dimension=0, tiled=True)
    return mixed.astype(jnp.bfloat16)


def solution(mesh):
    n_fsdp, n_tp = mesh.shape["fsdp"], mesh.shape["tp"]

    def body(tokens, gate_weight, up_weight, down_weight):
        hidden, width = gate_weight.shape
        every = tokens.shape[0] * n_fsdp
        resident = 6 * hidden * width + 24 * every * width + 48 * every * hidden
        if hidden % GROUP or hidden < GROUP * n_tp * LAG or every % 16 or resident > VMEM_BYTES:
            return collective_body(tokens, gate_weight, up_weight, down_weight)
        return fused_call(n_fsdp, n_tp, tokens, gate_weight, up_weight, down_weight)

    placed = (P("fsdp", "tp"),) * 4
    return jax.shard_map(
        body, mesh=mesh, in_specs=placed, out_specs=P("fsdp", "tp"), check_vma=False
    )
```

time: 122 us -> 42.3 us (0.35)
  blocking collectives: 47.7 us -> 0 us
  Pallas kernels: 0 us -> 40.7 us
  waiting for transfers between devices: 34.1 us -> 0 us
  matrix products: 19.7 us -> 0 us
  between operations: 14.6 us -> 0.01 us
  local copies, waits for them, and re-layouts: 3.26 us -> 1.3 us
  other arithmetic: 1.87 us -> 0 us
    pallas_call x0 -> x1, Pallas kernels: none -> 40.7 us  [fused_call(): pl.pallas_call(functools.partial(fused, n_fsdp, n_tp), out_shape=jax.Shap...]
    unnamed x2 -> x0, waiting for transfers between devices: 34.1 us -> none
    all_gather x2 -> x0, blocking collectives: 24.1 us -> none  [the longest x1 13.3 us: body(): hidden = lax.all_gather(quarter, 'tp', axis=0, tiled=True)]
    unnamed x1 -> x0, blocking collectives: 23.6 us -> none
    dot_general x3 -> x0, matrix products: 19.7 us -> none  [the longest x1 8.93 us: body(): lax.dot_general(block_rows, gate_weight, contract, preferred_element_type...]
    unnamed x6 -> x1, local copies, waits for them, and re-layouts: 2.65 us -> 1.3 us
  transfers between devices with their start and end apart: 1 -> 0, of which waited for: 1 -> 0; matrix products, arithmetic and copies ran while one was open for 2% -> 0% of each run, Pallas kernels for 0% -> 0%
where the time goes in v1:
time: 42.3 us; the launch traced here: 42 us
  Pallas kernels  40.7 us (96%)
  local copies, waits for them, and re-layouts  1.3 us (3%)
    pallas_call x1, Pallas kernels, fused_call(): pl.pallas_call(functools.partial(fused, n_fsdp, n_tp), out_shape=jax.Shap...  40.7 us
    unnamed x1, local copies, waits for them, and re-layouts  1.3 us

profile of v1, /device:TPU:0, one launch (start us, length us, event | category | flops | bytes accessed | tf_op | source)
XLA Modules:
  0.0 42.0 jit_solution(470849600968354830)
XLA Ops:
  0.0 40.7 %swiglu.1 = bf16[2,2048]{1,0:T(2,128)(2,1)} custom-call(bf16[2,2048]{1,0:T(2,128)(2,1)} %tokens.1, bf16[3456,2048]{1,0:T(8,128)(2,1)} %gate_w.1, bf16[3456,2048]{1,0:T(8,128)(2,1)} %up_w.1, bf16[3456,2048]{1,0:T(8,128)(2,1)} %down_w.1), custom_call_target="tpu_custom_call" | custom-call | flops 679477248 | bytes 42467328 | tf_op jit(solution)/shard_map/swiglu/pallas_call | solution.py:192
  40.7 1.3 %copy.6 = bf16[2,2048]{1,0:T(2,128)(2,1)} copy(bf16[2,2048]{1,0:T(2,128)(2,1)} %swiglu.1) | data formatting | bytes 16384

commit v2 on v1

--- a/solution.py
+++ b/solution.py
@@ -29,15 +29,18 @@
         return min(chunk, hidden - s * chunk)
 
     def load(k, source, target, s):
-        at = pl.ds(s * chunk, width(s))
+        size = chunk if not isinstance(s, int) else width(s)
+        at = pl.ds(s * chunk if isinstance(s, int) else pl.multiple_of(s * chunk, chunk), size)
         return pltpu.make_async_copy(source.at[at], target.at[at], w_sem.at[k, s])
 
-    for s in range(n_chunks):
+    def load_gate_up(s):
         load(0, gate_w, wg, s).start()
         load(1, up_w, wu, s).start()
-    for s in range(n_chunks):
+
+    def load_down(s):
         load(2, down_w, wd, s).start()
 
+    load_gate_up(0)
     own_copy = pltpu.make_async_copy(tokens, slots.at[f], own_sem)
     own_copy.start()
 
@@ -55,6 +58,7 @@
 
     for d in range(1, n_fsdp):
         tok_copy(d, f, lax.rem(f + d, n_fsdp)).start()
+    load_gate_up(1)
     own_copy.wait()
     for d in range(1, n_fsdp):
         tok_copy(d, lax.rem(f + n_fsdp - d, n_fsdp), f).wait_recv()
@@ -80,11 +84,50 @@
             hid.at[s, owner], hid.at[s, owner], h_send.at[s, d - 1], h_recv.at[s, d - 1],
             device_id={"tp": lax.rem(t + d, n_tp)}, device_id_type=MESH)
 
+    def load_ahead(s):
+        if isinstance(s, int):
+            load_down(2)
+            load_down(3)
+            return
+
+        @pl.when(s + 2 < full)
+        def _():
+            load_gate_up(s + 2)
+
+        @pl.when(s == full - 2)
+        def _():
+            if last_owners:
+                load_gate_up(full)
+            else:
+                load_down(2)
+
+        @pl.when(s == full - 1)
+        def _():
+            load_down(0)
+            load_down(1)
+            if not last_owners:
+                load_down(3)
+
+    def load_down_ahead(s):
+        if isinstance(s, int):
+            return
+
+        @pl.when(s + 4 < full)
+        def _():
+            load_down(s + 4)
+
+        if last_owners:
+            @pl.when(s + 4 == full)
+            def _():
+                load_down(full)
+
     def gate_up(s, owners):
         size = owners * GROUP
         at = pl.ds(pl.multiple_of(s * chunk, chunk), size)
         for k, (source, target) in enumerate(((gate_w, wg), (up_w, wu))):
             pltpu.make_async_copy(source.at[at], target.at[at], w_sem.at[k, s]).wait()
+        load_ahead(s)
+        for k, target in enumerate((wg, wu)):
             sums = lax.dot_general(x[...], target[at, :], NT, preferred_element_type=jnp.float32)
             for j in range(owners):
                 piece = sums[:, j * GROUP:(j + 1) * GROUP]
@@ -117,6 +160,7 @@
             when(True if owners == n_tp else owner < owners,
                  lambda d=d, owner=owner: hid_copy(s, d, owner).wait_recv())
         pltpu.make_async_copy(down_w.at[at], wd.at[at], w_sem.at[2, s]).wait()
+        load_down_ahead(s)
         h = jnp.concatenate([hid[s, j] for j in range(owners)], axis=1)
         acc[...] += jnp.dot(h, wd[at, :], preferred_element_type=jnp.float32)
 
@@ -164,7 +208,7 @@
     for d in range(1, n_fsdp):
         out_copy(d, f).wait_recv()
         total = total + land[d - 1]
-    out[...] = total.astype(out.dtype)
+    out[...] = total
 
     for d in range(1, n_fsdp):
         tok_copy(d, f, f).wait_send()
@@ -191,7 +235,7 @@
     any_spec = pl.BlockSpec(memory_space=pl.ANY)
     return pl.pallas_call(
         functools.partial(fused, n_fsdp, n_tp),
-        out_shape=jax.ShapeDtypeStruct((rows, width), tokens.dtype),
+        out_shape=jax.ShapeDtypeStruct((rows, width), jnp.float32),
         in_specs=[any_spec] * 4,
         out_specs=pl.BlockSpec(memory_space=pltpu.VMEM),
         scratch_shapes=[
@@ -225,7 +269,7 @@
             flops=6 * every * hidden * width, bytes_accessed=6 * hidden * width,
             transcendentals=every * hidden // n_tp),
         name="swiglu",
-    )(tokens, gate_w, up_w, down_w)
+    )(tokens, gate_w, up_w, down_w).astype(tokens.dtype)
 
 
 def collective_body(tokens, gate_weight, up_weight, down_weight):
@@ -251,7 +295,7 @@
         hidden, width = gate_weight.shape
         every = tokens.shape[0] * n_fsdp
         resident = 6 * hidden * width + 24 * every * width + 48 * every * hidden
-        if hidden % GROUP or hidden < GROUP * n_tp * LAG or every % 16 or resident > VMEM_BYTES:
+        if hidden % GROUP or hidden < GROUP * n_tp * 4 or every % 16 or resident > VMEM_BYTES:
             return collective_body(tokens, gate_weight, up_weight, down_weight)
         return fused_call(n_fsdp, n_tp, tokens, gate_weight, up_weight, down_weight)
 

time: 42.3 us -> 34.4 us (0.81)
  Pallas kernels: 40.7 us -> 32.9 us
  other arithmetic: 0 us -> 1.32 us
  local copies, waits for them, and re-layouts: 1.3 us -> 0 us
    pallas_call x1, Pallas kernels: 40.7 us -> 32.9 us  [fused_call(): pl.pallas_call(functools.partial(fused, n_fsdp, n_tp), out_shape=jax.Shap...]
    convert_element_type x0 -> x1, other arithmetic: none -> 1.32 us  [fused_call(): return pl.pallas_call(functools.partial(fused, n_fsdp, n_tp), out_shape=j...]
    unnamed x1 -> x0, local copies, waits for them, and re-layouts: 1.3 us -> none
where the time goes in v2:
time: 34.4 us; the launch traced here: 34.2 us
  Pallas kernels  32.9 us (96%)
  other arithmetic  1.32 us (4%)
    pallas_call x1, Pallas kernels, fused_call(): pl.pallas_call(functools.partial(fused, n_fsdp, n_tp), out_shape=jax.Shap...  32.9 us
    convert_element_type x1, other arithmetic, fused_call(): return pl.pallas_call(functools.partial(fused, n_fsdp, n_tp), out_shape=j...  1.32 us

profile of v2, /device:TPU:0, one launch (start us, length us, event | category | flops | bytes accessed | tf_op | source)
XLA Modules:
  0.0 34.2 jit_solution(12921150479328876319)
XLA Ops:
  0.0 32.9 %swiglu.1 = f32[2,2048]{1,0:T(2,128)} custom-call(bf16[2,2048]{1,0:T(2,128)(2,1)} %tokens.1, bf16[3456,2048]{1,0:T(8,128)(2,1)} %gate_w.1, bf16[3456,2048]{1,0:T(8,128)(2,1)} %up_w.1, bf16[3456,2048]{1,0:T(8,128)(2,1)} %down_w.1), custom_call_target="tpu_custom_call" | custom-call | flops 679477248 | bytes 42467328 | tf_op jit(solution)/shard_map/swiglu/pallas_call | solution.py:236
  32.9 1.3 %convert_element_type.3 = bf16[2,2048]{1,0:T(2,128)(2,1)} convert(f32[2,2048]{1,0:T(2,128)} %swiglu.1) | non-fusion elementwise | flops 4096 | bytes 24576 | tf_op jit(solution)/shard_map/convert_element_type | solution.py:272

commit v3 on v1

--- a/solution.py
+++ b/solution.py
@@ -9,7 +9,7 @@
 
 MESH = pl.DeviceIdType.MESH
 GROUP = 128
-LAG = 2
+LAG = 3
 WIRE = jnp.float32
 NT = (((1,), (1,)), ((), ()))
 VMEM_BYTES = 58 * 2**20
@@ -29,15 +29,16 @@
         return min(chunk, hidden - s * chunk)
 
     def load(k, source, target, s):
-        at = pl.ds(s * chunk, width(s))
+        size = chunk if not isinstance(s, int) else width(s)
+        at = pl.ds(s * chunk if isinstance(s, int) else pl.multiple_of(s * chunk, chunk), size)
         return pltpu.make_async_copy(source.at[at], target.at[at], w_sem.at[k, s])
 
-    for s in range(n_chunks):
-        load(0, gate_w, wg, s).start()
-        load(1, up_w, wu, s).start()
-    for s in range(n_chunks):
-        load(2, down_w, wd, s).start()
-
+    def start(k, s):
+        source, target = ((gate_w, wg), (up_w, wu), (down_w, wd))[k]
+        load(k, source, target, s).start(priority=1)
+
+    start(0, 0)
+    start(1, 0)
     own_copy = pltpu.make_async_copy(tokens, slots.at[f], own_sem)
     own_copy.start()
 
@@ -80,11 +81,28 @@
             hid.at[s, owner], hid.at[s, owner], h_send.at[s, d - 1], h_recv.at[s, d - 1],
             device_id={"tp": lax.rem(t + d, n_tp)}, device_id_type=MESH)
 
+    def start_next(k, s):
+        if isinstance(s, int):
+            start(2, k)
+            return
+
+        @pl.when(s + 1 < full)
+        def _():
+            start(k, s + 1)
+
+        @pl.when(s + 1 == full)
+        def _():
+            if last_owners:
+                start(k, full)
+            else:
+                start(2, k)
+
     def gate_up(s, owners):
         size = owners * GROUP
         at = pl.ds(pl.multiple_of(s * chunk, chunk), size)
         for k, (source, target) in enumerate(((gate_w, wg), (up_w, wu))):
             pltpu.make_async_copy(source.at[at], target.at[at], w_sem.at[k, s]).wait()
+            start_next(k, s)
             sums = lax.dot_general(x[...], target[at, :], NT, preferred_element_type=jnp.float32)
             for j in range(owners):
                 piece = sums[:, j * GROUP:(j + 1) * GROUP]
@@ -131,24 +149,21 @@
     if last_owners:
         gate_up(full, last_owners)
 
-    @pl.loop(full - LAG, full)
-    def _(s):
-        activate(s, n_tp)
-
-    early = min(2, full)
-
-    @pl.loop(0, early)
+    for s in range(LAG):
+        activate(full - LAG + s, n_tp)
+        start(2, s + 2)
+        if s:
+            down(s - 1, n_tp)
+    if last_owners:
+        activate(full, last_owners)
+    for s in range(LAG + 2, n_chunks):
+        start(2, s)
+
+    @pl.loop(LAG - 1, full)
     def _(s):
         down(s, n_tp)
 
     if last_owners:
-        activate(full, last_owners)
-
-    @pl.loop(early, full)
-    def _(s):
-        down(s, n_tp)
-
-    if last_owners:
         down(full, last_owners)
 
     def out_copy(d, peer):
@@ -164,7 +179,7 @@
     for d in range(1, n_fsdp):
         out_copy(d, f).wait_recv()
         total = total + land[d - 1]
-    out[...] = total.astype(out.dtype)
+    out[...] = total
 
     for d in range(1, n_fsdp):
         tok_copy(d, f, f).wait_send()
@@ -191,7 +206,7 @@
     any_spec = pl.BlockSpec(memory_space=pl.ANY)
     return pl.pallas_call(
         functools.partial(fused, n_fsdp, n_tp),
-        out_shape=jax.ShapeDtypeStruct((rows, width), tokens.dtype),
+        out_shape=jax.ShapeDtypeStruct((rows, width), jnp.float32),
         in_specs=[any_spec] * 4,
         out_specs=pl.BlockSpec(memory_space=pltpu.VMEM),
         scratch_shapes=[
@@ -225,7 +240,7 @@
             flops=6 * every * hidden * width, bytes_accessed=6 * hidden * width,
             transcendentals=every * hidden // n_tp),
         name="swiglu",
-    )(tokens, gate_w, up_w, down_w)
+    )(tokens, gate_w, up_w, down_w).astype(tokens.dtype)
 
 
 def collective_body(tokens, gate_weight, up_weight, down_weight):
@@ -251,7 +266,7 @@
         hidden, width = gate_weight.shape
         every = tokens.shape[0] * n_fsdp
         resident = 6 * hidden * width + 24 * every * width + 48 * every * hidden
-        if hidden % GROUP or hidden < GROUP * n_tp * LAG or every % 16 or resident > VMEM_BYTES:
+        if hidden % GROUP or hidden < GROUP * n_tp * (LAG + 2) or every % 16 or resident > VMEM_BYTES:
             return collective_body(tokens, gate_weight, up_weight, down_weight)
         return fused_call(n_fsdp, n_tp, tokens, gate_weight, up_weight, down_weight)
 

time: 42.3 us -> 34.2 us (0.81)
  Pallas kernels: 40.7 us -> 32.6 us
  other arithmetic: 0 us -> 1.32 us
  local copies, waits for them, and re-layouts: 1.3 us -> 0 us
    pallas_call x1, Pallas kernels: 40.7 us -> 32.6 us  [fused_call(): pl.pallas_call(functools.partial(fused, n_fsdp, n_tp), out_shape=jax.Shap...]
    convert_element_type x0 -> x1, other arithmetic: none -> 1.32 us  [fused_call(): return pl.pallas_call(functools.partial(fused, n_fsdp, n_tp), out_shape=j...]
    unnamed x1 -> x0, local copies, waits for them, and re-layouts: 1.3 us -> none
where the time goes in v3:
time: 34.2 us; the launch traced here: 33.9 us
  Pallas kernels  32.6 us (95%)
  other arithmetic  1.32 us (4%)
    pallas_call x1, Pallas kernels, fused_call(): pl.pallas_call(functools.partial(fused, n_fsdp, n_tp), out_shape=jax.Shap...  32.6 us
    convert_element_type x1, other arithmetic, fused_call(): return pl.pallas_call(functools.partial(fused, n_fsdp, n_tp), out_shape=j...  1.32 us

profile of v3, /device:TPU:0, one launch (start us, length us, event | category | flops | bytes accessed | tf_op | source)
XLA Modules:
  0.0 33.9 jit_solution(16219041787249384694)
XLA Ops:
  0.0 32.6 %swiglu.1 = f32[2,2048]{1,0:T(2,128)} custom-call(bf16[2,2048]{1,0:T(2,128)(2,1)} %tokens.1, bf16[3456,2048]{1,0:T(8,128)(2,1)} %gate_w.1, bf16[3456,2048]{1,0:T(8,128)(2,1)} %up_w.1, bf16[3456,2048]{1,0:T(8,128)(2,1)} %down_w.1), custom_call_target="tpu_custom_call" | custom-call | flops 679477248 | bytes 42467328 | tf_op jit(solution)/shard_map/swiglu/pallas_call | solution.py:207
  32.6 1.3 %convert_element_type.3 = bf16[2,2048]{1,0:T(2,128)(2,1)} convert(f32[2,2048]{1,0:T(2,128)} %swiglu.1) | non-fusion elementwise | flops 4096 | bytes 24576 | tf_op jit(solution)/shard_map/convert_element_type | solution.py:243

commit v4 on v3

--- a/solution.py
+++ b/solution.py
@@ -10,16 +10,18 @@
 MESH = pl.DeviceIdType.MESH
 GROUP = 128
 LAG = 3
-WIRE = jnp.float32
+OUT_PARTS = 2
+AHEAD = 4
 NT = (((1,), (1,)), ((), ()))
 VMEM_BYTES = 58 * 2**20
 
 
 def fused(n_fsdp, n_tp, tokens, gate_w, up_w, down_w, out,
-          wg, wu, wd, slots, xf, x, part, own, recv, hid, acc, send, land,
+          wg, wu, wd, slots, xf, x, part, recv, hid, acc, send, land,
           w_sem, own_sem, tok_send, tok_recv, p_send, p_recv, h_send, h_recv, o_send, o_recv):
     f, t = lax.axis_index("fsdp"), lax.axis_index("tp")
-    rows, hidden = tokens.shape[0], gate_w.shape[0]
+    (rows, whole), hidden = tokens.shape, gate_w.shape[0]
+    part_width = whole // OUT_PARTS
     chunk = GROUP * n_tp
     n_chunks = -(-hidden // chunk)
     full = hidden // chunk
@@ -36,6 +38,21 @@
     def start(k, s):
         source, target = ((gate_w, wg), (up_w, wu), (down_w, wd))[k]
         load(k, source, target, s).start(priority=1)
+
+    def start_down(s):
+        if isinstance(s, int):
+            if s < n_chunks:
+                start(2, s)
+            return
+
+        @pl.when(jnp.logical_and(s >= 0, s < full))
+        def _():
+            start(2, s)
+
+        if last_owners:
+            @pl.when(s == full)
+            def _():
+                start(2, full)
 
     start(0, 0)
     start(1, 0)
@@ -56,6 +73,9 @@
 
     for d in range(1, n_fsdp):
         tok_copy(d, f, lax.rem(f + d, n_fsdp)).start()
+    for s in range(1, AHEAD):
+        start(0, s)
+        start(1, s)
     own_copy.wait()
     for d in range(1, n_fsdp):
         tok_copy(d, lax.rem(f + n_fsdp - d, n_fsdp), f).wait_recv()
@@ -82,20 +102,17 @@
             device_id={"tp": lax.rem(t + d, n_tp)}, device_id_type=MESH)
 
     def start_next(k, s):
-        if isinstance(s, int):
-            start(2, k)
-            return
-
-        @pl.when(s + 1 < full)
-        def _():
-            start(k, s + 1)
-
-        @pl.when(s + 1 == full)
-        def _():
+        later = s + AHEAD
+        if not isinstance(s, int):
+            @pl.when(later < full)
+            def _():
+                start(k, later)
+
             if last_owners:
-                start(k, full)
-            else:
-                start(2, k)
+                @pl.when(later == full)
+                def _():
+                    start(k, full)
+        start_down(2 * (later - n_chunks) + k)
 
     def gate_up(s, owners):
         size = owners * GROUP
@@ -106,28 +123,24 @@
             sums = lax.dot_general(x[...], target[at, :], NT, preferred_element_type=jnp.float32)
             for j in range(owners):
                 piece = sums[:, j * GROUP:(j + 1) * GROUP]
-                part[s, j, k] = piece.astype(part.dtype)
-
-                @pl.when(t == j)
-                def _():
-                    own[s, k] = piece
+                part[s, j, k] = piece
         for d in range(1, n_tp):
             when(True if owners == n_tp else lax.rem(t + d, n_tp) < owners,
                  lambda d=d: part_copy(s, d).start())
 
     def activate(s, owners):
         def run():
-            gate, up = own[s, 0], own[s, 1]
+            gate, up = part[s, t, 0], part[s, t, 1]
             for d in range(1, n_tp):
                 part_copy(s, d).wait_recv()
-                gate = gate + recv[s, d - 1, 0].astype(jnp.float32)
-                up = up + recv[s, d - 1, 1].astype(jnp.float32)
+                gate = gate + recv[s, d - 1, 0]
+                up = up + recv[s, d - 1, 1]
             hid[s, t] = (gate / (1.0 + jnp.exp(-gate)) * up).astype(hid.dtype)
             for d in range(1, n_tp):
                 hid_copy(s, d, t).start()
         when(True if owners == n_tp else t < owners, run)
 
-    def down(s, owners):
+    def arrive(s, owners):
         size = owners * GROUP
         at = pl.ds(pl.multiple_of(s * chunk, chunk), size)
         for d in range(1, n_tp):
@@ -135,8 +148,22 @@
             when(True if owners == n_tp else owner < owners,
                  lambda d=d, owner=owner: hid_copy(s, d, owner).wait_recv())
         pltpu.make_async_copy(down_w.at[at], wd.at[at], w_sem.at[2, s]).wait()
+
+    def down(s, owners, first, last):
+        at = pl.ds(pl.multiple_of(s * chunk, chunk), owners * GROUP)
         h = jnp.concatenate([hid[s, j] for j in range(owners)], axis=1)
-        acc[...] += jnp.dot(h, wd[at, :], preferred_element_type=jnp.float32)
+        acc[:, first:last] += jnp.dot(h, wd[at, first:last], preferred_element_type=jnp.float32)
+
+    def out_copy(k, d, peer):
+        return pltpu.make_async_remote_copy(
+            send.at[k, peer], land.at[k, d - 1], o_send.at[k, d - 1], o_recv.at[k, d - 1],
+            device_id={"fsdp": peer}, device_id_type=MESH)
+
+    def send_out(k):
+        for p in range(n_fsdp):
+            send[k, p] = acc[p * rows:(p + 1) * rows, k * part_width:(k + 1) * part_width]
+        for d in range(1, n_fsdp):
+            out_copy(k, d, lax.rem(f + d, n_fsdp)).start()
 
     @pl.loop(0, full)
     def _(s):
@@ -149,41 +176,40 @@
     if last_owners:
         gate_up(full, last_owners)
 
+    for s in range(2 * AHEAD, n_chunks):
+        start_down(s)
     for s in range(LAG):
         activate(full - LAG + s, n_tp)
-        start(2, s + 2)
         if s:
-            down(s - 1, n_tp)
+            arrive(s - 1, n_tp)
+            down(s - 1, n_tp, 0, whole)
     if last_owners:
         activate(full, last_owners)
-    for s in range(LAG + 2, n_chunks):
-        start(2, s)
-
-    @pl.loop(LAG - 1, full)
+
+    @pl.loop(LAG - 1, full - 1)
     def _(s):
-        down(s, n_tp)
-
+        arrive(s, n_tp)
+        down(s, n_tp, 0, whole)
+
+    arrive(full - 1, n_tp)
     if last_owners:
-        down(full, last_owners)
-
-    def out_copy(d, peer):
-        return pltpu.make_async_remote_copy(
-            send.at[peer], land.at[d - 1], o_send.at[d - 1], o_recv.at[d - 1],
-            device_id={"fsdp": peer}, device_id_type=MESH)
-
-    for p in range(n_fsdp):
-        send[p] = acc[p * rows:(p + 1) * rows, :]
-    for d in range(1, n_fsdp):
-        out_copy(d, lax.rem(f + d, n_fsdp)).start()
-    total = send[f]
-    for d in range(1, n_fsdp):
-        out_copy(d, f).wait_recv()
-        total = total + land[d - 1]
-    out[...] = total
+        arrive(full, last_owners)
+    for k in range(OUT_PARTS):
+        down(full - 1, n_tp, k * part_width, (k + 1) * part_width)
+        if last_owners:
+            down(full, last_owners, k * part_width, (k + 1) * part_width)
+        send_out(k)
+    for k in range(OUT_PARTS):
+        total = send[k, f]
+        for d in range(1, n_fsdp):
+            out_copy(k, d, f).wait_recv()
+            total = total + land[k, d - 1]
+        out[:, k * part_width:(k + 1) * part_width] = total
 
     for d in range(1, n_fsdp):
         tok_copy(d, f, f).wait_send()
-        out_copy(d, f).wait_send()
+        for k in range(OUT_PARTS):
+            out_copy(k, d, f).wait_send()
 
     @pl.loop(0, full)
     def _(s):
@@ -216,13 +242,12 @@
             pltpu.VMEM((n_fsdp, rows, width), tokens.dtype),
             pltpu.VMEM((every, width), jnp.float32),
             pltpu.VMEM((every, width), tokens.dtype),
-            pltpu.VMEM((chunks, n_tp, 2, every, GROUP), WIRE),
-            pltpu.VMEM((chunks, 2, every, GROUP), jnp.float32),
-            pltpu.VMEM((chunks, n_tp - 1, 2, every, GROUP), WIRE),
+            pltpu.VMEM((chunks, n_tp, 2, every, GROUP), jnp.float32),
+            pltpu.VMEM((chunks, n_tp - 1, 2, every, GROUP), jnp.float32),
             pltpu.VMEM((chunks, n_tp, every, GROUP), jnp.bfloat16),
             pltpu.VMEM((every, width), jnp.float32),
-            pltpu.VMEM((n_fsdp, rows, width), jnp.float32),
-            pltpu.VMEM((n_fsdp - 1, rows, width), jnp.float32),
+            pltpu.VMEM((OUT_PARTS, n_fsdp, rows, width // OUT_PARTS), jnp.float32),
+            pltpu.VMEM((OUT_PARTS, n_fsdp - 1, rows, width // OUT_PARTS), jnp.float32),
             dma((3, chunks)),
             dma,
             dma((n_fsdp - 1,)),
@@ -231,8 +256,8 @@
             dma((chunks, n_tp - 1)),
             dma((chunks, n_tp - 1)),
             dma((chunks, n_tp - 1)),
-            dma((n_fsdp - 1,)),
-            dma((n_fsdp - 1,)),
+            dma((OUT_PARTS, n_fsdp - 1)),
+            dma((OUT_PARTS, n_fsdp - 1)),
         ],
         compiler_params=pltpu.CompilerParams(
             collective_id=0, has_side_effects=True, vmem_limit_bytes=VMEM_BYTES),
@@ -266,7 +291,7 @@
         hidden, width = gate_weight.shape
         every = tokens.shape[0] * n_fsdp
         resident = 6 * hidden * width + 24 * every * width + 48 * every * hidden
-        if hidden % GROUP or hidden < GROUP * n_tp * (LAG + 2) or every % 16 or resident > VMEM_BYTES:
+        if hidden % GROUP or hidden < GROUP * n_tp * (AHEAD + 2) or every % 16 or resident > VMEM_BYTES:
             return collective_body(tokens, gate_weight, up_weight, down_weight)
         return fused_call(n_fsdp, n_tp, tokens, gate_weight, up_weight, down_weight)
 

time: 34.2 us -> 33.6 us (0.982)
  Pallas kernels: 32.6 us -> 32 us
    pallas_call x1, Pallas kernels: 32.6 us -> 32 us  [fused_call(): pl.pallas_call(functools.partial(fused, n_fsdp, n_tp), out_shape=jax.Shap...]
where the time goes in v4:
time: 33.6 us; the launch traced here: 33.3 us
  Pallas kernels  32 us (95%)
  other arithmetic  1.32 us (4%)
    pallas_call x1, Pallas kernels, fused_call(): pl.pallas_call(functools.partial(fused, n_fsdp, n_tp), out_shape=jax.Shap...  32 us
    convert_element_type x1, other arithmetic, fused_call(): return pl.pallas_call(functools.partial(fused, n_fsdp, n_tp), out_shape=j...  1.32 us

profile of v4, /device:TPU:0, one launch (start us, length us, event | category | flops | bytes accessed | tf_op | source)
XLA Modules:
  0.0 33.3 jit_solution(11713138909672390442)
XLA Ops:
  0.0 32.0 %swiglu.1 = f32[2,2048]{1,0:T(2,128)} custom-call(bf16[2,2048]{1,0:T(2,128)(2,1)} %tokens.1, bf16[3456,2048]{1,0:T(8,128)(2,1)} %gate_w.1, bf16[3456,2048]{1,0:T(8,128)(2,1)} %up_w.1, bf16[3456,2048]{1,0:T(8,128)(2,1)} %down_w.1), custom_call_target="tpu_custom_call" | custom-call | flops 679477248 | bytes 42467328 | tf_op jit(solution)/shard_map/swiglu/pallas_call | solution.py:233
  32.0 1.3 %convert_element_type.3 = bf16[2,2048]{1,0:T(2,128)(2,1)} convert(f32[2,2048]{1,0:T(2,128)} %swiglu.1) | non-fusion elementwise | flops 4096 | bytes 24576 | tf_op jit(solution)/shard_map/convert_element_type | solution.py:268

commit v5 on v4

--- a/solution.py
+++ b/solution.py
@@ -12,15 +12,17 @@
 LAG = 3
 OUT_PARTS = 2
 AHEAD = 4
+WIRE = jnp.bfloat16
 NT = (((1,), (1,)), ((), ()))
 VMEM_BYTES = 58 * 2**20
 
 
 def fused(n_fsdp, n_tp, tokens, gate_w, up_w, down_w, out,
-          wg, wu, wd, slots, xf, x, part, recv, hid, acc, send, land,
+          wg, wu, wd, slots, xf, x, own, part, recv, hid, acc, send, land,
           w_sem, own_sem, tok_send, tok_recv, p_send, p_recv, h_send, h_recv, o_send, o_recv):
     f, t = lax.axis_index("fsdp"), lax.axis_index("tp")
     (rows, whole), hidden = tokens.shape, gate_w.shape[0]
+    every = rows * n_fsdp
     part_width = whole // OUT_PARTS
     chunk = GROUP * n_tp
     n_chunks = -(-hidden // chunk)
@@ -56,6 +58,7 @@
 
     start(0, 0)
     start(1, 0)
+    xf[...] = jnp.zeros_like(xf)
     own_copy = pltpu.make_async_copy(tokens, slots.at[f], own_sem)
     own_copy.start()
 
@@ -81,7 +84,7 @@
         tok_copy(d, lax.rem(f + n_fsdp - d, n_fsdp), f).wait_recv()
     for p in range(n_fsdp):
         xf[p * rows:(p + 1) * rows, :] = slots[p].astype(jnp.float32)
-    x[...] = xf[...].astype(x.dtype)
+    x[...] = xf[...].T.astype(x.dtype)
     acc[...] = jnp.zeros_like(acc)
 
     def when(cond, run):
@@ -120,21 +123,22 @@
         for k, (source, target) in enumerate(((gate_w, wg), (up_w, wu))):
             pltpu.make_async_copy(source.at[at], target.at[at], w_sem.at[k, s]).wait()
             start_next(k, s)
-            sums = lax.dot_general(x[...], target[at, :], NT, preferred_element_type=jnp.float32)
+            sums = jnp.dot(target[at, :], x[...], preferred_element_type=jnp.float32).T[:every]
             for j in range(owners):
                 piece = sums[:, j * GROUP:(j + 1) * GROUP]
-                part[s, j, k] = piece
+                own[s, j, k] = piece
+                part[s, j, k] = piece.astype(part.dtype)
         for d in range(1, n_tp):
             when(True if owners == n_tp else lax.rem(t + d, n_tp) < owners,
                  lambda d=d: part_copy(s, d).start())
 
     def activate(s, owners):
         def run():
-            gate, up = part[s, t, 0], part[s, t, 1]
+            gate, up = own[s, t, 0], own[s, t, 1]
             for d in range(1, n_tp):
                 part_copy(s, d).wait_recv()
-                gate = gate + recv[s, d - 1, 0]
-                up = up + recv[s, d - 1, 1]
+                gate = gate + recv[s, d - 1, 0].astype(jnp.float32)
+                up = up + recv[s, d - 1, 1].astype(jnp.float32)
             hid[s, t] = (gate / (1.0 + jnp.exp(-gate)) * up).astype(hid.dtype)
             for d in range(1, n_tp):
                 hid_copy(s, d, t).start()
@@ -240,10 +244,11 @@
             pltpu.VMEM((hidden, width), up_w.dtype),
             pltpu.VMEM((hidden, width), down_w.dtype),
             pltpu.VMEM((n_fsdp, rows, width), tokens.dtype),
-            pltpu.VMEM((every, width), jnp.float32),
-            pltpu.VMEM((every, width), tokens.dtype),
+            pltpu.VMEM((GROUP, width), jnp.float32),
+            pltpu.VMEM((width, GROUP), tokens.dtype),
             pltpu.VMEM((chunks, n_tp, 2, every, GROUP), jnp.float32),
-            pltpu.VMEM((chunks, n_tp - 1, 2, every, GROUP), jnp.float32),
+            pltpu.VMEM((chunks, n_tp, 2, every, GROUP), WIRE),
+            pltpu.VMEM((chunks, n_tp - 1, 2, every, GROUP), WIRE),
             pltpu.VMEM((chunks, n_tp, every, GROUP), jnp.bfloat16),
             pltpu.VMEM((every, width), jnp.float32),
             pltpu.VMEM((OUT_PARTS, n_fsdp, rows, width // OUT_PARTS), jnp.float32),
@@ -291,7 +296,7 @@
         hidden, width = gate_weight.shape
         every = tokens.shape[0] * n_fsdp
         resident = 6 * hidden * width + 24 * every * width + 48 * every * hidden
-        if hidden % GROUP or hidden < GROUP * n_tp * (AHEAD + 2) or every % 16 or resident > VMEM_BYTES:
+        if hidden % GROUP or hidden < GROUP * n_tp * (AHEAD + 2) or every % 16 or every > GROUP or resident > VMEM_BYTES:
             return collective_body(tokens, gate_weight, up_weight, down_weight)
         return fused_call(n_fsdp, n_tp, tokens, gate_weight, up_weight, down_weight)
 

time: 33.6 us -> 40.3 us (1.20)
  Pallas kernels: 32 us -> 38.7 us
    pallas_call x1, Pallas kernels: 32 us -> 38.7 us  [fused_call(): pl.pallas_call(functools.partial(fused, n_fsdp, n_tp), out_shape=jax.Shap...]
where the time goes in v5:
time: 40.3 us; the launch traced here: 40 us
  Pallas kernels  38.7 us (96%)
  other arithmetic  1.32 us (3%)
    pallas_call x1, Pallas kernels, fused_call(): pl.pallas_call(functools.partial(fused, n_fsdp, n_tp), out_shape=jax.Shap...  38.7 us
    convert_element_type x1, other arithmetic, fused_call(): return pl.pallas_call(functools.partial(fused, n_fsdp, n_tp), out_shape=j...  1.32 us

profile of v5, /device:TPU:0, one launch (start us, length us, event | category | flops | bytes accessed | tf_op | source)
XLA Modules:
  0.0 40.0 jit_solution(1620863164860923169)
XLA Ops:
  0.0 38.7 %swiglu.1 = f32[2,2048]{1,0:T(2,128)} custom-call(bf16[2,2048]{1,0:T(2,128)(2,1)} %tokens.1, bf16[3456,2048]{1,0:T(8,128)(2,1)} %gate_w.1, bf16[3456,2048]{1,0:T(8,128)(2,1)} %up_w.1, bf16[3456,2048]{1,0:T(8,128)(2,1)} %down_w.1), custom_call_target="tpu_custom_call" | custom-call | flops 679477248 | bytes 42467328 | tf_op jit(solution)/shard_map/swiglu/pallas_call | solution.py:237
  38.7 1.3 %convert_element_type.3 = bf16[2,2048]{1,0:T(2,128)(2,1)} convert(f32[2,2048]{1,0:T(2,128)} %swiglu.1) | non-fusion elementwise | flops 4096 | bytes 24576 | tf_op jit(solution)/shard_map/convert_element_type | solution.py:273

commit v6 on v4

--- a/solution.py
+++ b/solution.py
@@ -9,7 +9,8 @@
 
 MESH = pl.DeviceIdType.MESH
 GROUP = 128
-LAG = 3
+SPAN = 2
+LAG = 4
 OUT_PARTS = 2
 AHEAD = 4
 NT = (((1,), (1,)), ((), ()))
@@ -114,19 +115,24 @@
                     start(k, full)
         start_down(2 * (later - n_chunks) + k)
 
-    def gate_up(s, owners):
-        size = owners * GROUP
-        at = pl.ds(pl.multiple_of(s * chunk, chunk), size)
-        for k, (source, target) in enumerate(((gate_w, wg), (up_w, wu))):
-            pltpu.make_async_copy(source.at[at], target.at[at], w_sem.at[k, s]).wait()
-            start_next(k, s)
-            sums = lax.dot_general(x[...], target[at, :], NT, preferred_element_type=jnp.float32)
-            for j in range(owners):
-                piece = sums[:, j * GROUP:(j + 1) * GROUP]
-                part[s, j, k] = piece
-        for d in range(1, n_tp):
-            when(True if owners == n_tp else lax.rem(t + d, n_tp) < owners,
-                 lambda d=d: part_copy(s, d).start())
+    def gate_up(chunks, owners):
+        def at(s):
+            return pl.ds(pl.multiple_of(s * chunk, chunk), owners * GROUP)
+
+        for s in chunks:
+            for k, (source, target) in enumerate(((gate_w, wg), (up_w, wu))):
+                pltpu.make_async_copy(source.at[at(s)], target.at[at(s)], w_sem.at[k, s]).wait()
+                start_next(k, s)
+        sums = [[lax.dot_general(x[...], target[at(s), :], NT, preferred_element_type=jnp.float32)
+                 for target in (wg, wu)] for s in chunks]
+        for s, pair in zip(chunks, sums):
+            for k in range(2):
+                for j in range(owners):
+                    part[s, j, k] = pair[k][:, j * GROUP:(j + 1) * GROUP]
+        for s in chunks:
+            for d in range(1, n_tp):
+                when(True if owners == n_tp else lax.rem(t + d, n_tp) < owners,
+                     lambda s=s, d=d: part_copy(s, d).start())
 
     def activate(s, owners):
         def run():
@@ -165,16 +171,17 @@
         for d in range(1, n_fsdp):
             out_copy(k, d, lax.rem(f + d, n_fsdp)).start()
 
-    @pl.loop(0, full)
-    def _(s):
-        gate_up(s, n_tp)
-
-        @pl.when(s >= LAG)
+    @pl.loop(0, full // SPAN)
+    def _(i):
+        gate_up([i * SPAN + c for c in range(SPAN)], n_tp)
+
+        @pl.when(i * SPAN >= LAG)
         def _():
-            activate(s - LAG, n_tp)
+            for c in range(SPAN):
+                activate(i * SPAN + c - LAG, n_tp)
 
     if last_owners:
-        gate_up(full, last_owners)
+        gate_up([full], last_owners)
 
     for s in range(2 * AHEAD, n_chunks):
         start_down(s)
@@ -291,7 +298,7 @@
         hidden, width = gate_weight.shape
         every = tokens.shape[0] * n_fsdp
         resident = 6 * hidden * width + 24 * every * width + 48 * every * hidden
-        if hidden % GROUP or hidden < GROUP * n_tp * (AHEAD + 2) or every % 16 or resident > VMEM_BYTES:
+        if hidden % GROUP or hidden < GROUP * n_tp * (AHEAD + 2) or hidden // (GROUP * n_tp) % SPAN or every % 16 or resident > VMEM_BYTES:
             return collective_body(tokens, gate_weight, up_weight, down_weight)
         return fused_call(n_fsdp, n_tp, tokens, gate_weight, up_weight, down_weight)
 

time: 33.6 us -> 34.6 us (1.030)
  Pallas kernels: 32 us -> 33.1 us
    pallas_call x1, Pallas kernels: 32 us -> 33.1 us  [fused_call(): pl.pallas_call(functools.partial(fused, n_fsdp, n_tp), out_shape=jax.Shap...]
where the time goes in v6:
time: 34.6 us; the launch traced here: 34.4 us
  Pallas kernels  33.1 us (96%)
  other arithmetic  1.32 us (4%)
    pallas_call x1, Pallas kernels, fused_call(): pl.pallas_call(functools.partial(fused, n_fsdp, n_tp), out_shape=jax.Shap...  33.1 us
    convert_element_type x1, other arithmetic, fused_call(): return pl.pallas_call(functools.partial(fused, n_fsdp, n_tp), out_shape=j...  1.32 us

profile of v6, /device:TPU:0, one launch (start us, length us, event | category | flops | bytes accessed | tf_op | source)
XLA Modules:
  0.0 34.4 jit_solution(8019436177865488887)
XLA Ops:
  0.0 33.1 %swiglu.1 = f32[2,2048]{1,0:T(2,128)} custom-call(bf16[2,2048]{1,0:T(2,128)(2,1)} %tokens.1, bf16[3456,2048]{1,0:T(8,128)(2,1)} %gate_w.1, bf16[3456,2048]{1,0:T(8,128)(2,1)} %up_w.1, bf16[3456,2048]{1,0:T(8,128)(2,1)} %down_w.1), custom_call_target="tpu_custom_call" | custom-call | flops 679477248 | bytes 42467328 | tf_op jit(solution)/shard_map/swiglu/pallas_call | solution.py:240
  33.1 1.3 %convert_element_type.3 = bf16[2,2048]{1,0:T(2,128)(2,1)} convert(f32[2,2048]{1,0:T(2,128)} %swiglu.1) | non-fusion elementwise | flops 4096 | bytes 24576 | tf_op jit(solution)/shard_map/convert_element_type | solution.py:275
